TPU v7x, 128 devices: a whole 4x4x4 slice. The times are simulated.
128 devices in a mesh: row: 8 (over y_lo, x), col: 16 (over y_hi, z, core).
Axes of the slice: x: 4, y: 4 (y_hi: 2, y_lo: 2; y = y_hi * 2 + y_lo), z: 4, core: 2. Of those that a mesh axis runs over, the one named last changes fastest.
Arguments:
- spectra: float32 [2, 4, 30, 16, 512], P(None, None, None, 'col', 'row'), may hold values from -500 to 500
- counts: int32 [16, 512], P('col', 'row'), may hold values from 1 to 30
Outputs:
- stacks: float32 [16, 512, 9, 2, 4, 512], P('col', 'row')
All inputs are finite; a program needn't handle non-finite values.
Results may differ from a plain program's by a relative error of at most 0.004.
Values may be sent and summed in bfloat16 or wider, within the bound.
A program may use at most 64 MiB of HBM per device.

v0:
```python
import functools

import jax
import jax.numpy as jnp
from jax import lax
from jax.experimental import pallas as pl
from jax.experimental.pallas import tpu as pltpu
from jax.sharding import PartitionSpec as P

MESH = pl.DeviceIdType.MESH
BINS = 4
SEGS = 30
USED = 2 * BINS * SEGS
COLS = 256
WIDTH = 64
HALF = 32
HOPS = 9
SEL = 16


def gather_kernel(spec_in, cnt_in, g, lhs, rci, spec, cnt, own, ssem, rsem, lsem):
    fetch = (
        pltpu.make_async_copy(spec_in, spec, lsem.at[1]),
        pltpu.make_async_copy(cnt_in, cnt, lsem.at[2]),
    )
    for copy in fetch:
        copy.start()
    r, d = lax.axis_index("row"), lax.axis_index("col")
    x, ylo = r % 4, r // 4
    c, q = d % 2, d // 2
    z, yhi = q % 4, q // 4

    def dev(x_, ylo_, q_, c_):
        return (ylo_ * 4 + x_, q_ * 2 + c_)

    sibling = dev(x, ylo, q, 1 - c)
    other = 1 - ylo

    def at_y(rel):
        return other if rel else ylo

    plane = [(0, 1)] + [(j, rel) for j in range(1, 5) for rel in (0, 1)]

    barrier = pltpu.get_barrier_semaphore()
    sources = [dev(x, at_y(rel), (q + j) % 8, c) for j, rel in plane]
    sources += [dev((x + i) % 4, ylo, q, c) for i in (1, 2, 3)]
    sources += [dev(x, ylo, yhi * 4 + (z + e) % 4, c) for e in (1, 2, 3)]
    sources += [sibling]
    for source in sources:
        pl.semaphore_signal(barrier, inc=1, device_id=source, device_id_type=MESH)

    for copy in fetch:
        copy.wait()
    raw = spec[...]
    power = jnp.sum(raw * raw, axis=0, keepdims=True) / float(USED)
    row = lax.broadcasted_iota(jnp.int32, (USED, WIDTH), 0)
    group = jnp.zeros((USED, WIDTH), jnp.int32)
    for n in range(1, 2 * BINS):
        group = group + (row >= n * SEGS).astype(jnp.int32)
    valid = (row - SEGS * group < cnt[...]).astype(jnp.float32)
    white = raw * lax.rsqrt(power + 1e-6) * valid
    white = white.astype(jnp.bfloat16).astype(jnp.float32)
    count = cnt[...].astype(jnp.float32)
    pad = jnp.zeros((COLS - USED - 8, WIDTH), jnp.float32)
    first = lax.broadcasted_iota(jnp.int32, (8, WIDTH), 0) == 0
    tail = jnp.where(first, count, 0.0)
    straight = jnp.concatenate([white, tail, pad], axis=0).T
    own[...] = straight.astype(jnp.bfloat16)

    def remote(src, dst, device, send, recv):
        copy = pltpu.make_async_remote_copy(
            src_ref=src,
            dst_ref=dst,
            send_sem=ssem.at[send],
            recv_sem=rsem.at[recv],
            device_id=device,
            device_id_type=MESH,
        )
        copy.start()
        return copy

    def settle(region, sem):
        pltpu.make_async_copy(region, region, sem).wait()

    lo, hi = pl.ds(0, HALF), pl.ds(HALF, HALF)
    own_blocks = pl.ds(0, 5)

    pl.semaphore_wait(barrier, len(sources))
    for i in (1, 3, 2):
        remote(own.at[hi], g.at[0, ylo, x, hi], dev((x + i) % 4, ylo, q, c), 0, 0)
    for j, rel in plane:
        remote(own.at[lo], g.at[j, ylo, x, lo], dev(x, at_y(rel), (q - j) % 8, c), 1, 1)
    local = pltpu.make_async_copy(own, g.at[0, ylo, x], lsem.at[0])
    local.start()

    local.wait()

    settle(g.at[pl.ds(0, 3), 0, 0, hi], rsem.at[0])
    row = g.at[0, ylo, :, hi]
    for j, rel in ((4, 1), (0, 1), (4, 0)):
        remote(row, g.at[j, ylo, :, hi], dev(x, at_y(rel), (q - j) % 8, c), 2, 2)

    right, left = dev((x + 1) % 4, ylo, q, c), dev((x + 3) % 4, ylo, q, c)
    settle(g.at[pl.ds(0, 9), 0, 0, lo], rsem.at[1])
    columns = [g.at[own_blocks, rel, x, lo] for rel in (0, 1)]
    to_right = [remote(columns[0], columns[0], right, 3, 3)]
    to_left = {1: remote(columns[1], columns[1], left, 3, 4)}
    to_right.append(remote(columns[1], columns[1], right, 3, 5))
    to_left[0] = remote(columns[0], columns[0], left, 3, 6)

    def share(src_index, dst_index, recv):
        remote(g.at[src_index], g.at[dst_index], sibling, 5, recv)

    def share_column(column):
        share((pl.ds(1 - c, 4), slice(None), column, lo), (pl.ds(5, 4), slice(None), column, lo), 12)

    def share_block(j):
        at = 4 + j + c
        share((j, slice(None), slice(None), hi), (at, slice(None), slice(None), hi), 12)

    settle(g.at[pl.ds(0, 3), 0, :, hi], rsem.at[2])
    along_z = {}
    for e in (1, 3, 2):
        zt = (z + 4 - e) % 4
        block = jnp.where(zt > z, 4, 0)
        along_z[e] = remote(
            g.at[block, :, :, hi], g.at[e, :, :, hi], dev(x, ylo, yhi * 4 + zt, c), 4, 6 + e
        )
    share_column(x)
    share_block(4 * (1 - c))

    xl, xr, xo = (x + 3) % 4, (x + 1) % 4, (x + 2) % 4
    to_right[0].wait_recv()
    piece = g.at[own_blocks, 0, xl, lo]
    on_right = remote(piece, piece, right, 3, 10)
    to_left[1].wait_recv()
    piece = g.at[own_blocks, 1, xr, lo]
    on_left = remote(piece, piece, left, 3, 11)
    to_right[1].wait_recv()
    share_column(xl)
    to_left[0].wait_recv()
    share_column(xr)
    swapped = jnp.concatenate(
        [white[USED // 2 :], -white[: USED // 2], jnp.zeros((COLS - USED, WIDTH), jnp.float32)],
        axis=0,
    ).T
    shape = (WIDTH, 8, COLS)
    sub = lax.broadcasted_iota(jnp.int32, (8, COLS), 0)
    lane = lax.broadcasted_iota(jnp.int32, (8, COLS), 1)
    low = (sub % BINS) * SEGS
    here = ((lane >= low) & (lane < low + SEGS)) | (
        (lane >= low + USED // 2) & (lane < low + USED // 2 + SEGS)
    )
    one = jnp.broadcast_to(straight[:, None, :], shape)
    two = jnp.broadcast_to(swapped[:, None, :], shape)
    sel = lax.broadcasted_iota(jnp.int32, (SEL, COLS), 1) == USED
    for odd in (0, 1):
        pick = jnp.where(((sub < BINS) == (odd == 0))[None], one, two)
        pick = jnp.where(here[None], pick, 0.0)
        lhs[odd, :SEL, :] = sel.astype(jnp.float32).astype(jnp.bfloat16)
        lhs[odd, SEL:, :] = pick.reshape(WIDTH * 8, COLS).astype(jnp.bfloat16)
    mine = jnp.broadcast_to(1.0 / straight[:, USED : USED + 1], (WIDTH, 128))
    rci[...] = jnp.broadcast_to(mine[:, None, :], (WIDTH, 8, 128)).reshape(WIDTH * 8, 128)

    for e in (1, 3):
        along_z[e].wait_recv()
        share_block(e)
    on_right.wait_recv()
    on_left.wait_recv()
    share_column(xo)
    along_z[2].wait_recv()
    share_block(2)

    settle(g.at[pl.ds(5, 4)], rsem.at[12])
    settle(g.at[pl.ds(0, 3), 0, 0, hi], ssem.at[0])
    settle(g.at[pl.ds(0, 9), 0, 0, lo], ssem.at[1])
    settle(g.at[pl.ds(0, 3), 0, :, hi], ssem.at[2])
    settle(g.at[pl.ds(0, 5), 0, pl.ds(0, 3)], ssem.at[3])
    settle(g.at[pl.ds(0, 3), :, :, hi], ssem.at[4])
    settle(g.at[pl.ds(5, 4)], ssem.at[5])


def stack_kernel(g, lhs, rci, out, stage, sems):
    mine = rci[...]

    def held(k):
        return jnp.where(k % 2 == 0, k // 2, 5 + k // 2)

    def to_out(k):
        return pltpu.make_async_copy(stage.at[k], out.at[:, k], sems.at[k])

    @pl.loop(0, HOPS)
    def _(k):
        def tiles(odd):
            first = 128 * odd
            right = [g[held(k), at : at + 128, :] for at in (first, first + 256)]
            result = lax.dot_general(
                lhs[odd],
                jnp.concatenate(right, axis=0),
                (((1,), (1,)), ((), ())),
                preferred_element_type=jnp.float32,
            )
            recip = 1.0 / result[0:1]
            halves = (slice(0, 128), slice(128, 256))
            return [
                (result[SEL:, lanes] * jnp.maximum(mine, recip[:, lanes])).reshape(WIDTH, 8, 128)
                for lanes in halves
            ]

        lower = lax.broadcasted_iota(jnp.int32, (WIDTH, 8, 128), 1) < BINS
        for n, (even, odd) in enumerate(zip(tiles(0), tiles(1))):
            rows = pl.ds(8 * n, 8)
            stage[k, :, 0, rows] = jnp.where(lower, even, odd)
            stage[k, :, 1, rows] = pltpu.roll(jnp.where(lower, odd, even), BINS, 1)
        to_out(k).start()

    @pl.loop(0, HOPS)
    def _(k):
        to_out(k).wait()


def per_device(spectra, counts):
    spec = spectra.reshape(USED, WIDTH)
    vmem = pl.BlockSpec(memory_space=pltpu.VMEM)
    hbm = pl.BlockSpec(memory_space=pltpu.HBM)
    g, lhs, rci = pl.pallas_call(
        gather_kernel,
        name="whiten_gather",
        out_shape=(
            jax.ShapeDtypeStruct((HOPS, 2, 4, WIDTH, COLS), jnp.bfloat16),
            jax.ShapeDtypeStruct((2, SEL + WIDTH * 8, COLS), jnp.bfloat16),
            jax.ShapeDtypeStruct((WIDTH * 8, 128), jnp.float32),
        ),
        in_specs=[hbm, hbm],
        out_specs=(vmem, vmem, vmem),
        scratch_shapes=[
            pltpu.VMEM((USED, WIDTH), jnp.float32),
            pltpu.VMEM((1, WIDTH), jnp.int32),
            pltpu.VMEM((WIDTH, COLS), jnp.bfloat16),
            pltpu.SemaphoreType.DMA((6,)),
            pltpu.SemaphoreType.DMA((13,)),
            pltpu.SemaphoreType.DMA((3,)),
        ],
        compiler_params=pltpu.CompilerParams(
            collective_id=0, has_side_effects=True, vmem_limit_bytes=16 * 2**20
        ),
    )(*(pltpu.with_memory_space_constraint(a, pltpu.HBM) for a in (spec, counts)))
    g = g.reshape(HOPS, 512, COLS)
    out = pl.pallas_call(
        stack_kernel,
        name="stack",
        out_shape=jax.ShapeDtypeStruct((WIDTH, HOPS, 2, 4 * BINS, 128), jnp.float32),
        in_specs=[vmem, vmem, vmem],
        out_specs=hbm,
        scratch_shapes=[
            pltpu.VMEM((HOPS, WIDTH, 2, 4 * BINS, 128), jnp.float32),
            pltpu.SemaphoreType.DMA((HOPS,)),
        ],
        compiler_params=pltpu.CompilerParams(vmem_limit_bytes=24 * 2**20),
        cost_estimate=pl.CostEstimate(
            flops=2 * (SEL + WIDTH * 8) * COLS * 512 * HOPS,
            bytes_accessed=HOPS * 512 * (COLS * 2 + WIDTH * 8 * 4),
            transcendentals=0,
        ),
    )(g, lhs, rci)
    out = out.reshape(WIDTH, HOPS, 2, 4, BINS, 128).swapaxes(3, 4)
    return out.reshape(1, WIDTH, HOPS, 2, BINS, 512)


def solution(mesh):
    return jax.shard_map(
        per_device,
        mesh=mesh,
        in_specs=(P(None, None, None, "col", "row"), P("col", "row")),
        out_specs=P("col", "row", None, None, None, None),
        check_vma=False,
    )
```

profile of v0, /device:TPU:1, one launch (start us, length us, event | category | flops | bytes accessed | tf_op | source)
XLA Modules:
  0.0 28.1 jit_solution(1448034670678108827)
XLA Ops:
  0.0 23.9 %whiten_gather.1 = (bf16[9,2,4,64,256]{4,3,2,1,0:T(8,128)(2,1)S(1)}, bf16[2,528,256]{2,1,0:T(8,128)(2,1)S(1)}, f32[512,128]{1,0:T(8,128)S(1)}) custom-call(f32[240,64]{1,0:T(8,128)} %bitcast.8, s32[1,64]{1,0:T(1,128)} %cnt_in.1), custom_call_target="tpu_custom_call" | custom-call | tf_op jit(solution)/shard_map/whiten_gather/pallas_call | solution.py:226
  23.9 4.2 %stack.1 = f32[64,9,2,16,128]{4,3,2,1,0:T(8,128)} custom-call(bf16[9,512,256]{2,1,0:T(8,128)(2,1)S(1)} %bitcast.7, bf16[2,528,256]{2,1,0:T(8,128)(2,1)S(1)} %get-tuple-element.9.lhs, f32[512,128]{1,0:T(8,128)S(1)} %get-tuple-element.10.rci), custom_call_target="tpu_custom_call" | custom-call | flops 1245708288 | bytes 11796480 | tf_op jit(solution)/shard_map/stack/pallas_call | solution.py:249
where the time goes:
time: 28.2 us; the launch traced here: 28.1 us
  Pallas kernels  28.1 us (100%)
    pallas_call x1, Pallas kernels, per_device(): pl.pallas_call(gather_kernel, name='whiten_gather', out_shape=(jax.ShapeD...  23.9 us
    pallas_call x1, Pallas kernels, per_device(): pl.pallas_call(stack_kernel, name='stack', out_shape=jax.ShapeDtypeStruct...  4.16 us

commit v1 on v0

--- a/solution.py
+++ b/solution.py
@@ -39,7 +39,7 @@
     def at_y(rel):
         return other if rel else ylo
 
-    plane = [(0, 1)] + [(j, rel) for j in range(1, 5) for rel in (0, 1)]
+    plane = [(j, rel) for j in (2, 4, 1, 3, 0) for rel in (0, 1) if j or rel]
 
     barrier = pltpu.get_barrier_semaphore()
     sources = [dev(x, at_y(rel), (q + j) % 8, c) for j, rel in plane]
@@ -86,7 +86,7 @@
     own_blocks = pl.ds(0, 5)
 
     pl.semaphore_wait(barrier, len(sources))
-    for i in (1, 3, 2):
+    for i in (2, 1, 3):
         remote(own.at[hi], g.at[0, ylo, x, hi], dev((x + i) % 4, ylo, q, c), 0, 0)
     for j, rel in plane:
         remote(own.at[lo], g.at[j, ylo, x, lo], dev(x, at_y(rel), (q - j) % 8, c), 1, 1)
@@ -97,7 +97,7 @@
 
     settle(g.at[pl.ds(0, 3), 0, 0, hi], rsem.at[0])
     row = g.at[0, ylo, :, hi]
-    for j, rel in ((4, 1), (0, 1), (4, 0)):
+    for j, rel in ((4, 0), (4, 1), (0, 1)):
         remote(row, g.at[j, ylo, :, hi], dev(x, at_y(rel), (q - j) % 8, c), 2, 2)
 
     right, left = dev((x + 1) % 4, ylo, q, c), dev((x + 3) % 4, ylo, q, c)
@@ -118,15 +118,16 @@
         at = 4 + j + c
         share((j, slice(None), slice(None), hi), (at, slice(None), slice(None), hi), 12)
 
+    share_column(x)
+
     settle(g.at[pl.ds(0, 3), 0, :, hi], rsem.at[2])
     along_z = {}
-    for e in (1, 3, 2):
+    for e in (2, 1, 3):
         zt = (z + 4 - e) % 4
         block = jnp.where(zt > z, 4, 0)
         along_z[e] = remote(
             g.at[block, :, :, hi], g.at[e, :, :, hi], dev(x, ylo, yhi * 4 + zt, c), 4, 6 + e
         )
-    share_column(x)
     share_block(4 * (1 - c))
 
     xl, xr, xo = (x + 3) % 4, (x + 1) % 4, (x + 2) % 4
@@ -189,7 +190,7 @@
     def to_out(k):
         return pltpu.make_async_copy(stage.at[k], out.at[:, k], sems.at[k])
 
-    @pl.loop(0, HOPS)
+    @pl.loop(0, HOPS, unroll=3)
     def _(k):
         def tiles(odd):
             first = 128 * odd

time: 28.2 us -> 27.6 us (0.979)
  Pallas kernels: 28.1 us -> 27.4 us
    pallas_call x1, Pallas kernels: 23.9 us -> 23.4 us  [per_device(): pl.pallas_call(gather_kernel, name='whiten_gather', out_shape=(jax.ShapeD...]
where the time goes in v1:
time: 27.6 us; the launch traced here: 27.5 us
  Pallas kernels  27.4 us (99%)
    pallas_call x1, Pallas kernels, per_device(): pl.pallas_call(gather_kernel, name='whiten_gather', out_shape=(jax.ShapeD...  23.4 us
    pallas_call x1, Pallas kernels, per_device(): pl.pallas_call(stack_kernel, name='stack', out_shape=jax.ShapeDtypeStruct...  4.06 us

profile of v1, /device:TPU:1, one launch (start us, length us, event | category | flops | bytes accessed | tf_op | source)
XLA Modules:
  0.0 27.5 jit_solution(2073570136342113183)
XLA Ops:
  0.0 23.4 %whiten_gather.1 = (bf16[9,2,4,64,256]{4,3,2,1,0:T(8,128)(2,1)S(1)}, bf16[2,528,256]{2,1,0:T(8,128)(2,1)S(1)}, f32[512,128]{1,0:T(8,128)S(1)}) custom-call(f32[240,64]{1,0:T(8,128)} %bitcast.8, s32[1,64]{1,0:T(1,128)} %cnt_in.1), custom_call_target="tpu_custom_call" | custom-call | tf_op jit(solution)/shard_map/whiten_gather/pallas_call | solution.py:227
  23.4 4.1 %stack.1 = f32[64,9,2,16,128]{4,3,2,1,0:T(8,128)} custom-call(bf16[9,512,256]{2,1,0:T(8,128)(2,1)S(1)} %bitcast.7, bf16[2,528,256]{2,1,0:T(8,128)(2,1)S(1)} %get-tuple-element.9.lhs, f32[512,128]{1,0:T(8,128)S(1)} %get-tuple-element.10.rci), custom_call_target="tpu_custom_call" | custom-call | flops 1245708288 | bytes 11796480 | tf_op jit(solution)/shard_map/stack/pallas_call | solution.py:250
